TPU v7x, 32 devices: a whole 2x2x4 slice. The times are simulated.
32 devices in a mesh: gx: 8 (over z, y), gy: 4 (over x, core).
Axes of the slice: x: 2, y: 2, z: 4, core: 2. Of those that a mesh axis runs over, the one named last changes fastest.
Arguments:
- increment: float32 [1, 90, 384, 512], P(None, None, 'gx', 'gy'), may hold values from -6 to 6
- covariances: float32 [19, 90, 90], replicated, may hold values from 0 to 8, as said below
Outputs:
- weighted: float32 [1, 90, 384, 512], P(None, None, 'gx', 'gy')
Inputs may be any that keep to these rules, and one draw needn't show every extreme that they name: `covariances`: one matrix of order 90 for each subband, of order one up to a factor that grows with the subband's level.
All inputs are finite; a program needn't handle non-finite values.
Results may differ from a plain program's by a relative error of at most 0.0001.
Values sent between devices are 32-bit elements; how exact they have to be, the bound alone decides.
A program may use at most 128 MiB of HBM per device.

v0:
```python
import functools

import jax
import jax.numpy as jnp
from jax import lax
from jax.experimental import pallas as pl
from jax.experimental.pallas import tpu as pltpu
from jax.sharding import PartitionSpec as P

LEVELS = 6
HANDOVER = 4
LANES = 128
COLS = 8
AHEAD = 6
BACK = {1: 4, 2: 6, 3: 6, 4: 6, 5: 6, 6: 6}
SENT = {1: 3, 2: 5, 3: 6}
MESH = pl.DeviceIdType.MESH

LOW_TAPS = (
    0.2303778133088964,
    0.7148465705529155,
    0.6308807679298587,
    -0.0279837694168599,
    -0.1870348117190931,
    0.0308413818355607,
    0.0328830116668852,
    -0.010597401785069,
)
HIGH_TAPS = (
    -0.010597401785069,
    -0.0328830116668852,
    0.0308413818355607,
    0.1870348117190931,
    -0.0279837694168599,
    -0.6308807679298587,
    0.7148465705529154,
    -0.2303778133088964,
)


def rows_loop(first, last, body):
    def step(r, carry):
        body(r)
        return carry

    lax.fori_loop(first, last, step, 0)


def split_rows(source, work, rows, cols):
    def body(k):
        smooth = detail = None
        for j in range(8):
            row = source[2 * k + j, 0:cols, :]
            if j == 0:
                smooth, detail = LOW_TAPS[j] * row, HIGH_TAPS[j] * row
            else:
                smooth, detail = smooth + LOW_TAPS[j] * row, detail + HIGH_TAPS[j] * row
        work[0, k, 0:cols, :] = smooth
        work[1, k, 0:cols, :] = detail

    rows_loop(0, rows, body)


def split_cols(work, rows, half, put):
    def body(k):
        for side in range(2):
            smooth = detail = None
            for j in range(8):
                part = work[side, k, pl.ds(j, half, stride=2), :]
                if j == 0:
                    smooth, detail = LOW_TAPS[j] * part, HIGH_TAPS[j] * part
                else:
                    smooth, detail = smooth + LOW_TAPS[j] * part, detail + HIGH_TAPS[j] * part
            put(side, k, smooth, detail)

    rows_loop(0, rows, body)


def halves(values):
    upper = values.astype(jnp.bfloat16)
    lower = (values - upper.astype(jnp.float32)).astype(jnp.bfloat16)
    return upper, lower


def product(values, upper, lower):
    first, second = halves(values)
    dot = functools.partial(jnp.dot, preferred_element_type=jnp.float32)
    return dot(first, upper) + (dot(second, upper) + dot(first, lower))


def mix(ref, band, cov, index, row0, rows, col0, cols):
    upper, lower = halves(cov[index])
    chunk = 1
    for c in range(1, rows + 1):
        if rows % c == 0 and c * cols <= 512:
            chunk = c

    def body(r):
        at = (band, pl.ds(row0 + r * chunk, chunk), slice(col0, col0 + cols), slice(None))
        values = ref[at].reshape(chunk * cols, LANES)
        ref[at] = product(values, upper, lower).reshape(chunk, cols, LANES)

    rows_loop(0, rows // chunk, body)


def merge_level(smooth, bands, work, out, back, first_row, rows, cols, out_cols, out_rows):
    count = cols + out_cols // 2
    start = COLS - out_cols // 2

    def along_y(r):
        for side in range(2):
            if side == 0:
                left, right = smooth.at[r], bands.at[0, r]
            else:
                left, right = bands.at[1, r], bands.at[2, r]
            even = odd = None
            for t in range(4):
                s = left[start - t:start - t + count, :]
                d = right[start - t:start - t + count, :]
                e = LOW_TAPS[2 * t] * s + HIGH_TAPS[2 * t] * d
                o = LOW_TAPS[2 * t + 1] * s + HIGH_TAPS[2 * t + 1] * d
                even, odd = (e, o) if t == 0 else (even + e, odd + o)
            work[side, r, pl.ds(0, count, stride=2), :] = even
            work[side, r, pl.ds(1, count, stride=2), :] = odd

    rows_loop(first_row, back + rows, along_y)
    width = 2 * cols + out_cols

    def along_x(n):
        even = odd = None
        for t in range(4):
            at = n - out_rows // 2 - t + back
            s = work[0, at, 0:width, :]
            d = work[1, at, 0:width, :]
            e = LOW_TAPS[2 * t] * s + HIGH_TAPS[2 * t] * d
            o = LOW_TAPS[2 * t + 1] * s + HIGH_TAPS[2 * t + 1] * d
            even, odd = (e, o) if t == 0 else (even + e, odd + o)
        out[2 * n, 0:width, :] = even
        out[2 * n + 1, 0:width, :] = odd

    rows_loop(0, rows + out_rows // 2, along_x)


def fill(ref):
    ref[...] = jnp.zeros(ref.shape, jnp.float32)


def kernel(nx, ny, X, Y, back_x, back_y, inc, cov, out, *scratch):
    (a0, a1, a2, a3, m1, m2, m3, s4, m4, g4, e4, e5, top, m5, m6, r6, r5, r4, r4l, r3, r2, r1,
     work, load_sem, a_send, a_recv, m_send, m_recv, s_send, s_recv, g_send, g_recv) = scratch
    approx = (a0, a1, a2, a3)
    mixed = {1: m1, 2: m2, 3: m3}
    gx, gy = lax.axis_index("gx"), lax.axis_index("gy")
    total = nx * ny
    me = gx * ny + gy
    X4, Y4 = X[4], Y[4]

    load = pltpu.make_async_copy(inc, a0.at[0:X[0], 0:Y[0]], load_sem)
    load.start()

    def place(o):
        other = lax.rem(me + o, total)
        return (lax.div(other, ny), lax.rem(other, ny))

    barrier = pltpu.get_barrier_semaphore()

    def greet(o):
        pl.semaphore_signal(barrier, inc=1, device_id=place(o), device_id_type=MESH)

    rows_loop(1, total, greet)
    pl.semaphore_wait(barrier, total - 1)

    sends = []

    def move(source, target, send_sem, recv_sem, dx, dy):
        def copy():
            return pltpu.make_async_remote_copy(
                src_ref=source, dst_ref=target, send_sem=send_sem, recv_sem=recv_sem,
                device_id=(gx + dx, gy + dy), device_id_type=MESH)

        def inside(px, py):
            terms = []
            if dx:
                terms += [px >= 0, px < nx]
            if dy:
                terms += [py >= 0, py < ny]
            return functools.reduce(jnp.logical_and, terms)

        gives, takes = inside(gx + dx, gy + dy), inside(gx - dx, gy - dy)

        @pl.when(gives)
        def _():
            copy().start()

        def sent():
            @pl.when(gives)
            def _():
                copy().wait_send()

        sends.append(sent)

        @pl.when(jnp.logical_not(takes))
        def _():
            fill(target)

        def arrive():
            @pl.when(takes)
            def _():
                copy().wait_recv()

        return arrive

    def send_ahead(level):
        ref, n, w = approx[level], X[level], Y[level]
        src = inc if level == 0 else ref
        own = ((slice(0, AHEAD), slice(0, w)), (slice(0, n), slice(0, COLS)), (slice(0, AHEAD), slice(0, COLS)))
        put = ((slice(n, n + AHEAD), slice(0, w)), (slice(0, n), slice(w, w + COLS)),
               (slice(n, n + AHEAD), slice(w, w + COLS)))
        way = ((-1, 0), (0, -1), (-1, -1))
        return [move(src.at[own[i]], ref.at[put[i]], a_send.at[3 * level + i], a_recv.at[3 * level + i], *way[i])
                for i in range(3)]

    def send_back(level):
        ref, n, w, b, s = mixed[level], X[level], Y[level], BACK[level], SENT[level]
        every = slice(0, 3)
        own = ((every, slice(b + n - s, b + n), slice(COLS, COLS + w)),
               (every, slice(b, b + n), slice(w, w + COLS)),
               (every, slice(b + n - s, b + n), slice(w, w + COLS)))
        put = ((every, slice(b - s, b), slice(COLS, COLS + w)),
               (every, slice(b, b + n), slice(0, COLS)),
               (every, slice(b - s, b), slice(0, COLS)))
        way = ((1, 0), (0, 1), (1, 1))
        base = 3 * (level - 1)
        return [move(ref.at[own[i]], ref.at[put[i]], m_send.at[base + i], m_recv.at[base + i], *way[i])
                for i in range(3)]

    arrivals = send_ahead(0)
    load.wait()
    late = {}
    for level in range(1, HANDOVER + 1):
        for arrive in arrivals:
            arrive()
        rows, cols = X[level], Y[level]
        split_rows(approx[level - 1], work, rows, Y[level - 1] + COLS)
        if level < HANDOVER:
            target, bands, b = approx[level], mixed[level], BACK[level]

            def put(side, k, smooth, detail):
                if side == 0:
                    target[k, 0:cols, :] = smooth
                    bands[0, b + k, COLS:COLS + cols, :] = detail
                else:
                    bands[1, b + k, COLS:COLS + cols, :] = smooth
                    bands[2, b + k, COLS:COLS + cols, :] = detail

            split_cols(work, rows, cols, put)
            arrivals = send_ahead(level)
            for band in range(3):
                mix(bands, band, cov, 3 * (level - 1) + band, b, rows, COLS, cols)
            late[level] = send_back(level)
        else:
            own4 = s4.at[0]
            if Y4 != COLS:
                fill(own4)
                fill(g4.at[me])

            def put(side, k, smooth, detail):
                if side == 0:
                    g4[me, k, 0:cols, :] = smooth
                    own4[0, k, 0:cols, :] = detail
                else:
                    own4[1, k, 0:cols, :] = smooth
                    own4[2, k, 0:cols, :] = detail

            split_cols(work, rows, cols, put)

    def spread(o):
        return pltpu.make_async_remote_copy(
            src_ref=g4.at[me], dst_ref=g4.at[me], send_sem=g_send.at[o], recv_sem=g_recv.at[o],
            device_id=place(o), device_id_type=MESH)

    def landed(o):
        return pltpu.make_async_remote_copy(
            src_ref=g4.at[me], dst_ref=g4.at[lax.rem(me + total - o, total)],
            send_sem=g_send.at[o], recv_sem=g_recv.at[o], device_id=place(o), device_id_type=MESH)

    rows_loop(1, total, lambda o: spread(o).start())

    for band in range(3):
        mix(s4.at[0], band, cov, 3 * (HANDOVER - 1) + band, 0, X4, 0, COLS)
    late4 = []
    for dx in range(back_x + 1):
        for dy in range(back_y + 1):
            if dx or dy:
                slot = dx * (back_y + 1) + dy
                late4.append(move(s4.at[0], s4.at[slot], s_send.at[slot], s_recv.at[slot], dx, dy))

    for ref in (e4, e5, m5, m6, r6):
        fill(ref)
    rows_loop(1, total, lambda o: landed(o).wait_recv())

    def assemble(px):
        for py in range(ny):
            for k in range(X4):
                e4[px * X4 + k, py * Y4:(py + 1) * Y4, :] = g4[px * ny + py, k, 0:Y4, :]

    rows_loop(0, nx, assemble)

    for level, source, target, bands in ((5, e4, e5, m5), (6, e5, top, m6)):
        rows, cols = X[level], Y[level]
        b = BACK[level]
        split_rows(source, work, rows, 2 * cols + COLS)

        def put(side, k, smooth, detail, target=target, bands=bands, b=b, cols=cols):
            if side == 0:
                if target is top:
                    r6[b + k, COLS:COLS + cols, :] = smooth
                else:
                    target[k, 0:cols, :] = smooth
                bands[0, b + k, COLS:COLS + cols, :] = detail
            else:
                bands[1, b + k, COLS:COLS + cols, :] = smooth
                bands[2, b + k, COLS:COLS + cols, :] = detail

        split_cols(work, rows, cols, put)
        for band in range(3):
            mix(bands, band, cov, 3 * (level - 1) + band, b, rows, COLS, cols)
    top[0] = r6[...]
    mix(top, 0, cov, 3 * LEVELS, BACK[6], X[6], COLS, Y[6])
    merge_level(top.at[0], m6, work, r5, BACK[6], 0, X[6], Y[6], COLS, BACK[5])
    merge_level(r5, m5, work, r4, BACK[5], 0, X[5], Y[5], COLS, BACK[4])

    for py in range(ny):
        @pl.when(gy == py)
        def _():
            def body(r):
                r4l[r, :, :] = r4[gx * X4 + r, py * Y4:py * Y4 + COLS + Y4, :]

            rows_loop(0, BACK[4] + X4, body)

    for arrive in late4:
        arrive()
    for dx in range(back_x + 1):
        for dy in range(back_y + 1):
            slot = dx * (back_y + 1) + dy
            row, col = BACK[4] - dx * X4, COLS - dy * Y4
            m4[:, row:row + X4, col:col + Y4, :] = s4[slot, :, :, 0:Y4, :]

    merge_level(r4l, m4, work, r3, BACK[4], 0, X4, Y4, COLS, BACK[3])
    for level, source, target in ((3, r3, r2), (2, r2, r1), (1, r1, out)):
        for arrive in late[level]:
            arrive()
        final = level == 1
        merge_level(source, mixed[level], work, target, BACK[level], BACK[level] - SENT[level], X[level], Y[level],
                    0 if final else COLS, 0 if final else BACK[level - 1])

    for sent in sends:
        sent()
    rows_loop(1, total, lambda o: spread(o).wait_send())


def per_device(nx, ny, increment, covariances):
    members, heights, block_x, block_y = increment.shape
    bands = covariances.shape[0]
    X = [block_x >> l for l in range(HANDOVER + 1)]
    Y = [block_y >> l for l in range(HANDOVER + 1)]
    wide_x, wide_y = nx * X[4], ny * Y[4]
    X += [wide_x // 2, wide_x // 4]
    Y += [wide_y // 2, wide_y // 4]
    back_x, back_y = BACK[4] // X[4], COLS // Y[4]
    extra = LANES - heights
    field = jnp.pad(jnp.transpose(increment[0], (1, 2, 0)), ((0, 0), (0, 0), (0, extra)))
    turned = jnp.pad(jnp.transpose(covariances, (0, 2, 1)), ((0, 0), (0, extra), (0, extra)))

    f32 = functools.partial(pltpu.VMEM, dtype=jnp.float32)

    def ahead(l):
        return f32((X[l] + AHEAD, Y[l] + COLS, LANES))

    def behind(l):
        return f32((BACK[l] + X[l], COLS + Y[l], LANES))

    def three(l):
        return f32((3, BACK[l] + X[l], COLS + Y[l], LANES))

    slots = (back_x + 1) * (back_y + 1)
    work_rows = max(X[1] + BACK[1], X[5] + BACK[5])
    work_cols = max(Y[0], wide_y) + COLS
    dma = pltpu.SemaphoreType.DMA
    scratch = [
        ahead(0), ahead(1), ahead(2), ahead(3),
        three(1), three(2), three(3),
        f32((slots, 3, X[4], COLS, LANES)), three(4),
        f32((nx * ny, X[4], COLS, LANES)),
        f32((wide_x + AHEAD, wide_y + COLS, LANES)), ahead(5),
        f32((1, BACK[6] + X[6], COLS + Y[6], LANES)),
        three(5), three(6), behind(6), behind(5),
        f32((BACK[4] + wide_x, COLS + wide_y, LANES)),
        behind(4), behind(3), behind(2), behind(1),
        f32((2, work_rows, work_cols, LANES)),
        dma, dma((12,)), dma((12,)), dma((9,)), dma((9,)), dma((slots,)), dma((slots,)),
        dma((nx * ny,)), dma((nx * ny,)),
    ]
    result = pl.pallas_call(
        functools.partial(kernel, nx, ny, X, Y, back_x, back_y),
        out_shape=jax.ShapeDtypeStruct((block_x, block_y, LANES), jnp.float32),
        in_specs=[pl.BlockSpec(memory_space=pl.ANY), pl.BlockSpec(memory_space=pltpu.VMEM)],
        out_specs=pl.BlockSpec(memory_space=pltpu.VMEM),
        scratch_shapes=scratch,
        compiler_params=pltpu.CompilerParams(
            collective_id=0, has_side_effects=True, vmem_limit_bytes=48 * 1024 * 1024),
    )(field, turned)
    return jnp.transpose(result[:, :, :heights], (2, 0, 1))[None]


def solution(mesh):
    nx, ny = mesh.shape["gx"], mesh.shape["gy"]
    placed = (P(None, None, "gx", "gy"), P())
    return jax.shard_map(
        functools.partial(per_device, nx, ny), mesh=mesh, in_specs=placed,
        out_specs=P(None, None, "gx", "gy"), check_vma=False)
```

profile of v0, /device:TPU:31, one launch (start us, length us, event | category | flops | bytes accessed | tf_op | source)
XLA Modules:
  0.0 83.9 jit_solution(7680111909614971835)
XLA Ops:
  0.0 1.6 %copy.4 = f32[19,90,90]{1,2,0:T(8,128)S(1)} copy(f32[19,90,90]{2,1,0:T(8,128)} %param.3) | data formatting | bytes 1231200 | tf_op args[1]
  1.6 0.1 pad.9.cov
  1.7 3.4 %copy.3 = f32[1,90,48,128]{1,3,2,0:T(8,128)} copy(f32[1,90,48,128]{3,2,1,0:T(8,128)} %param.2) | data formatting | bytes 4423680 | tf_op args[0]
  5.1 4.0 %pad.8.inc = f32[48,128,128]{2,1,0:T(8,128)} pad(f32[48,128,90]{2,1,0:T(8,128)} %bitcast.8, f32[]{:T(128)} %constant.2.clone.1), padding=0_0x0_0x0_38 | pad | bytes 5357572 | tf_op jit(solution)/shard_map/jit(_pad)/pad | solution.py:372
  9.1 72.3 %shard_map.28 = f32[48,128,128]{2,1,0:T(8,128)S(1)} custom-call(f32[48,128,128]{2,1,0:T(8,128)} %pad.8.inc, f32[19,128,128]{2,1,0:T(8,128)S(1)} %pad.9.cov), custom_call_target="tpu_custom_call" | custom-call | tf_op jit(solution)/shard_map/pallas_call | solution.py:404
  81.4 0.2 slice_bitcast_fusion
  81.6 2.2 %copy.5 = f32[1,90,48,128]{3,2,1,0:T(8,128)} copy(f32[1,90,48,128]{1,3,2,0:T(8,128)S(1)} %slice_bitcast_fusion) | data formatting | bytes 4423680 | tf_op jit(solution)/shard_map/broadcast_in_dim | solution.py:413
where the time goes:
time: 84.1 us; the launch traced here: 83.9 us
  Pallas kernels  72.3 us (86%)
  local copies, waits for them, and re-layouts  11.5 us (14%)
    pallas_call x1, Pallas kernels, per_device(): pl.pallas_call(functools.partial(kernel, nx, ny, X, Y, back_x, back_y), o...  72.3 us
    unnamed x2, local copies, waits for them, and re-layouts  5 us
    pad x1, local copies, waits for them, and re-layouts, per_device(): jnp.pad(jnp.transpose(increment[0], (1, 2, 0)), ((0, 0), (0, 0), (0, extr...  3.96 us
    broadcast_in_dim x2, local copies, waits for them, and re-layouts, per_device(): return jnp.transpose(result[:, :, :heights], (2, 0, 1))[None]  2.44 us

commit v1 on v0

--- a/solution.py
+++ b/solution.py
@@ -141,13 +141,18 @@
     rows_loop(0, rows + out_rows // 2, along_x)
 
 
+def turn(ref, row, steps, planes):
+    slab = ref.reshape(planes * steps, ref.shape[2])[pl.ds(row, planes, stride=steps), :]
+    return jnp.concatenate([slab, jnp.zeros((LANES - planes, slab.shape[1]), jnp.float32)]).T
+
+
 def fill(ref):
     ref[...] = jnp.zeros(ref.shape, jnp.float32)
 
 
 def kernel(nx, ny, X, Y, back_x, back_y, inc, cov, out, *scratch):
-    (a0, a1, a2, a3, m1, m2, m3, s4, m4, g4, e4, e5, top, m5, m6, r6, r5, r4, r4l, r3, r2, r1,
-     work, load_sem, a_send, a_recv, m_send, m_recv, s_send, s_recv, g_send, g_recv) = scratch
+    (raw, raw_ahead, a0, a1, a2, a3, m1, m2, m3, s4, m4, g4, e4, e5, top, m5, m6, r6, r5, r4, r4l, r3, r2, r1,
+     work, load_sem, a_send, a_recv, m_send, m_recv, s_send, s_recv, g_send, g_recv, pair_send, pair_recv) = scratch
     approx = (a0, a1, a2, a3)
     mixed = {1: m1, 2: m2, 3: m3}
     gx, gy = lax.axis_index("gx"), lax.axis_index("gy")
@@ -155,7 +160,11 @@
     me = gx * ny + gy
     X4, Y4 = X[4], Y[4]
 
-    load = pltpu.make_async_copy(inc, a0.at[0:X[0], 0:Y[0]], load_sem)
+    heights, planes = inc.shape[0], raw.shape[0]
+    chips, wide = total // 2, ny // 2
+    chip, core = gx * wide + lax.div(gy, 2), lax.rem(gy, 2)
+
+    load = pltpu.make_async_copy(inc, raw.at[0:heights], load_sem)
     load.start()
 
     def place(o):
@@ -168,11 +177,14 @@
         pl.semaphore_signal(barrier, inc=1, device_id=place(o), device_id_type=MESH)
 
     rows_loop(1, total, greet)
+    if planes > heights:
+        fill(raw.at[heights:planes])
+        fill(raw_ahead.at[heights:planes])
     pl.semaphore_wait(barrier, total - 1)
 
     sends = []
 
-    def move(source, target, send_sem, recv_sem, dx, dy):
+    def move(source, target, send_sem, recv_sem, dx, dy, absent=None, present=None):
         def copy():
             return pltpu.make_async_remote_copy(
                 src_ref=source, dst_ref=target, send_sem=send_sem, recv_sem=recv_sem,
@@ -201,24 +213,25 @@
 
         @pl.when(jnp.logical_not(takes))
         def _():
-            fill(target)
+            (absent or (lambda: fill(target)))()
 
         def arrive():
             @pl.when(takes)
             def _():
                 copy().wait_recv()
+                if present:
+                    present()
 
         return arrive
 
     def send_ahead(level):
         ref, n, w = approx[level], X[level], Y[level]
-        src = inc if level == 0 else ref
         own = ((slice(0, AHEAD), slice(0, w)), (slice(0, n), slice(0, COLS)), (slice(0, AHEAD), slice(0, COLS)))
         put = ((slice(n, n + AHEAD), slice(0, w)), (slice(0, n), slice(w, w + COLS)),
                (slice(n, n + AHEAD), slice(w, w + COLS)))
         way = ((-1, 0), (0, -1), (-1, -1))
-        return [move(src.at[own[i]], ref.at[put[i]], a_send.at[3 * level + i], a_recv.at[3 * level + i], *way[i])
-                for i in range(3)]
+        return [move(ref.at[own[i]], ref.at[put[i]], a_send.at[3 * level + i], a_recv.at[3 * level + i], *way[i])
+                for i in range(1 if level == 0 else 0, 3)]
 
     def send_back(level):
         ref, n, w, b, s = mixed[level], X[level], Y[level], BACK[level], SENT[level]
@@ -234,8 +247,19 @@
         return [move(ref.at[own[i]], ref.at[put[i]], m_send.at[base + i], m_recv.at[base + i], *way[i])
                 for i in range(3)]
 
-    arrivals = send_ahead(0)
+    def turn_ahead():
+        for r in range(AHEAD):
+            a0[X[0] + r, 0:Y[0], :] = turn(raw_ahead, r, COLS, planes)
+
+    first = move(inc.at[:, 0:AHEAD, :], raw_ahead.at[0:heights, 0:AHEAD, :], a_send.at[0], a_recv.at[0], -1, 0,
+                 lambda: fill(a0.at[X[0]:X[0] + AHEAD, 0:Y[0]]), turn_ahead)
     load.wait()
+
+    def turn_own(r):
+        a0[r, 0:Y[0], :] = turn(raw, r, X[0], planes)
+
+    rows_loop(0, X[0], turn_own)
+    arrivals = send_ahead(0) + [first]
     late = {}
     for level in range(1, HANDOVER + 1):
         for arrive in arrivals:
@@ -262,11 +286,11 @@
             own4 = s4.at[0]
             if Y4 != COLS:
                 fill(own4)
-                fill(g4.at[me])
+                fill(g4.at[core, chip])
 
             def put(side, k, smooth, detail):
                 if side == 0:
-                    g4[me, k, 0:cols, :] = smooth
+                    g4[core, chip, k, 0:cols, :] = smooth
                     own4[0, k, 0:cols, :] = detail
                 else:
                     own4[1, k, 0:cols, :] = smooth
@@ -275,16 +299,22 @@
             split_cols(work, rows, cols, put)
 
     def spread(o):
+        other = lax.rem(chip + o, chips)
         return pltpu.make_async_remote_copy(
-            src_ref=g4.at[me], dst_ref=g4.at[me], send_sem=g_send.at[o], recv_sem=g_recv.at[o],
-            device_id=place(o), device_id_type=MESH)
+            src_ref=g4.at[core, chip], dst_ref=g4.at[core, chip], send_sem=g_send.at[o], recv_sem=g_recv.at[o],
+            device_id=(lax.div(other, wide), 2 * lax.rem(other, wide) + core), device_id_type=MESH)
 
     def landed(o):
         return pltpu.make_async_remote_copy(
-            src_ref=g4.at[me], dst_ref=g4.at[lax.rem(me + total - o, total)],
-            send_sem=g_send.at[o], recv_sem=g_recv.at[o], device_id=place(o), device_id_type=MESH)
-
-    rows_loop(1, total, lambda o: spread(o).start())
+            src_ref=g4.at[core, chip], dst_ref=g4.at[core, lax.rem(chip + chips - o, chips)],
+            send_sem=g_send.at[o], recv_sem=g_recv.at[o], device_id=(gx, gy + 1 - 2 * core), device_id_type=MESH)
+
+    def pair(side):
+        return pltpu.make_async_remote_copy(
+            src_ref=g4.at[side], dst_ref=g4.at[side], send_sem=pair_send, recv_sem=pair_recv,
+            device_id=(gx, gy + 1 - 2 * core), device_id_type=MESH)
+
+    rows_loop(1, chips, lambda o: spread(o).start())
 
     for band in range(3):
         mix(s4.at[0], band, cov, 3 * (HANDOVER - 1) + band, 0, X4, 0, COLS)
@@ -297,12 +327,14 @@
 
     for ref in (e4, e5, m5, m6, r6):
         fill(ref)
-    rows_loop(1, total, lambda o: landed(o).wait_recv())
+    rows_loop(1, chips, lambda o: landed(o).wait_recv())
+    pair(core).start()
+    pair(1 - core).wait_recv()
 
     def assemble(px):
         for py in range(ny):
             for k in range(X4):
-                e4[px * X4 + k, py * Y4:(py + 1) * Y4, :] = g4[px * ny + py, k, 0:Y4, :]
+                e4[px * X4 + k, py * Y4:(py + 1) * Y4, :] = g4[py % 2, px * wide + py // 2, k, 0:Y4, :]
 
     rows_loop(0, nx, assemble)
 
@@ -356,7 +388,8 @@
 
     for sent in sends:
         sent()
-    rows_loop(1, total, lambda o: spread(o).wait_send())
+    rows_loop(1, chips, lambda o: spread(o).wait_send())
+    pair(core).wait_send()
 
 
 def per_device(nx, ny, increment, covariances):
@@ -369,7 +402,7 @@
     Y += [wide_y // 2, wide_y // 4]
     back_x, back_y = BACK[4] // X[4], COLS // Y[4]
     extra = LANES - heights
-    field = jnp.pad(jnp.transpose(increment[0], (1, 2, 0)), ((0, 0), (0, 0), (0, extra)))
+    planes = -(-heights // 8) * 8
     turned = jnp.pad(jnp.transpose(covariances, (0, 2, 1)), ((0, 0), (0, extra), (0, extra)))
 
     f32 = functools.partial(pltpu.VMEM, dtype=jnp.float32)
@@ -388,10 +421,11 @@
     work_cols = max(Y[0], wide_y) + COLS
     dma = pltpu.SemaphoreType.DMA
     scratch = [
+        f32((planes, block_x, block_y)), f32((planes, COLS, block_y)),
         ahead(0), ahead(1), ahead(2), ahead(3),
         three(1), three(2), three(3),
         f32((slots, 3, X[4], COLS, LANES)), three(4),
-        f32((nx * ny, X[4], COLS, LANES)),
+        f32((2, nx * ny // 2, X[4], COLS, LANES)),
         f32((wide_x + AHEAD, wide_y + COLS, LANES)), ahead(5),
         f32((1, BACK[6] + X[6], COLS + Y[6], LANES)),
         three(5), three(6), behind(6), behind(5),
@@ -399,7 +433,7 @@
         behind(4), behind(3), behind(2), behind(1),
         f32((2, work_rows, work_cols, LANES)),
         dma, dma((12,)), dma((12,)), dma((9,)), dma((9,)), dma((slots,)), dma((slots,)),
-        dma((nx * ny,)), dma((nx * ny,)),
+        dma((nx * ny // 2,)), dma((nx * ny // 2,)), dma, dma,
     ]
     result = pl.pallas_call(
         functools.partial(kernel, nx, ny, X, Y, back_x, back_y),
@@ -409,7 +443,7 @@
         scratch_shapes=scratch,
         compiler_params=pltpu.CompilerParams(
             collective_id=0, has_side_effects=True, vmem_limit_bytes=48 * 1024 * 1024),
-    )(field, turned)
+    )(increment[0], turned)
     return jnp.transpose(result[:, :, :heights], (2, 0, 1))[None]
 
 

time: 84.1 us -> 81.3 us (0.967)
  local copies, waits for them, and re-layouts: 11.5 us -> 9.25 us
    broadcast_in_dim x2, local copies, waits for them, and re-layouts: 2.44 us -> 7.36 us  [per_device(): return jnp.transpose(result[:, :, :heights], (2, 0, 1))[None]]
    pad x1 -> x0, local copies, waits for them, and re-layouts: 3.96 us -> none  [per_device(): jnp.pad(jnp.transpose(increment[0], (1, 2, 0)), ((0, 0), (0, 0), (0, extr...]
    unnamed x2 -> x3, local copies, waits for them, and re-layouts: 5 us -> 1.76 us
where the time goes in v1:
time: 81.3 us; the launch traced here: 81 us
  Pallas kernels  71.7 us (88%)
  local copies, waits for them, and re-layouts  9.25 us (11%)
    pallas_call x1, Pallas kernels, per_device(): pl.pallas_call(functools.partial(kernel, nx, ny, X, Y, back_x, back_y), o...  71.7 us
    broadcast_in_dim x2, local copies, waits for them, and re-layouts, per_device(): return jnp.transpose(result[:, :, :heights], (2, 0, 1))[None]  7.36 us
    unnamed x3, local copies, waits for them, and re-layouts  1.76 us

profile of v1, /device:TPU:31, one launch (start us, length us, event | category | flops | bytes accessed | tf_op | source)
XLA Modules:
  0.0 81.0 jit_solution(7388342962373178055)
XLA Ops:
  0.0 0.0 copy-start
  0.0 1.7 %copy.3 = f32[19,90,90]{1,2,0:T(8,128)S(1)} copy(f32[19,90,90]{2,1,0:T(8,128)} %param.3) | data formatting | bytes 1231200 | tf_op args[1]
  1.7 0.1 pad.4.cov
  1.9 0.0 copy-done
  1.9 71.7 %shard_map.28 = f32[48,128,128]{2,1,0:T(8,128)} custom-call(f32[90,48,128]{2,1,0:T(8,128)S(1)} %bitcast.6, f32[19,128,128]{2,1,0:T(8,128)S(1)} %pad.4.cov), custom_call_target="tpu_custom_call" | custom-call | tf_op jit(solution)/shard_map/pallas_call | solution.py:438
  73.6 3.9 %slice_bitcast_fusion = f32[1,90,48,128]{1,3,2,0:T(8,128)} fusion(f32[48,128,128]{2,1,0:T(8,128)} %shard_map.28), kind=kLoop, calls=%fused_computation | loop fusion | bytes 4423680 | tf_op jit(solution)/shard_map/broadcast_in_dim | solution.py:447
  77.6 3.4 %copy.4 = f32[1,90,48,128]{3,2,1,0:T(8,128)} copy(f32[1,90,48,128]{1,3,2,0:T(8,128)} %slice_bitcast_fusion) | data formatting | bytes 4423680 | tf_op jit(solution)/shard_map/broadcast_in_dim | solution.py:447
Async XLA Ops:
  0.0 1.9 %copy-start = (f32[1,90,48,128]{3,2,1,0:T(8,128)S(1)}, f32[1,90,48,128]{3,2,1,0:T(8,128)}, u32[]{:S(2)}) copy-start(f32[1,90,48,128]{3,2,1,0:T(8,128)} %param.2) | copy-start | bytes 6635524

commit v2 on v1

--- a/solution.py
+++ b/solution.py
@@ -10,6 +10,7 @@
 LEVELS = 6
 HANDOVER = 4
 LANES = 128
+UNROLL_A, UNROLL_B, UNROLL_C, UNROLL_T = 2, 4, 4, 8
 COLS = 8
 AHEAD = 6
 BACK = {1: 4, 2: 6, 3: 6, 4: 6, 5: 6, 6: 6}
@@ -38,12 +39,17 @@
 )
 
 
-def rows_loop(first, last, body):
+def rows_loop(first, last, body, unroll=1):
+    whole = (last - first) // unroll
+
     def step(r, carry):
+        for u in range(unroll):
+            body(first + r * unroll + u)
+        return carry
+
+    lax.fori_loop(0, whole, step, 0)
+    for r in range(first + whole * unroll, last):
         body(r)
-        return carry
-
-    lax.fori_loop(first, last, step, 0)
 
 
 def split_rows(source, work, rows, cols):
@@ -58,7 +64,7 @@
         work[0, k, 0:cols, :] = smooth
         work[1, k, 0:cols, :] = detail
 
-    rows_loop(0, rows, body)
+    rows_loop(0, rows, body, UNROLL_A)
 
 
 def split_cols(work, rows, half, put):
@@ -73,7 +79,7 @@
                     smooth, detail = smooth + LOW_TAPS[j] * part, detail + HIGH_TAPS[j] * part
             put(side, k, smooth, detail)
 
-    rows_loop(0, rows, body)
+    rows_loop(0, rows, body, UNROLL_B)
 
 
 def halves(values):
@@ -84,23 +90,25 @@
 
 def product(values, upper, lower):
     first, second = halves(values)
-    dot = functools.partial(jnp.dot, preferred_element_type=jnp.float32)
+    dot = functools.partial(
+        lax.dot_general, dimension_numbers=(((1,), (1,)), ((), ())), preferred_element_type=jnp.float32)
     return dot(first, upper) + (dot(second, upper) + dot(first, lower))
 
 
 def mix(ref, band, cov, index, row0, rows, col0, cols):
     upper, lower = halves(cov[index])
+    heights = cov.shape[1]
     chunk = 1
     for c in range(1, rows + 1):
         if rows % c == 0 and c * cols <= 512:
             chunk = c
 
     def body(r):
-        at = (band, pl.ds(row0 + r * chunk, chunk), slice(col0, col0 + cols), slice(None))
-        values = ref[at].reshape(chunk * cols, LANES)
-        ref[at] = product(values, upper, lower).reshape(chunk, cols, LANES)
-
-    rows_loop(0, rows // chunk, body)
+        at = (band, pl.ds(row0 + r * chunk, chunk), slice(col0, col0 + cols), slice(0, heights))
+        values = ref[at].reshape(chunk * cols, heights)
+        ref[at] = product(values, upper, lower).reshape(chunk, cols, heights)
+
+    rows_loop(0, rows // chunk, body, UNROLL_C)
 
 
 def merge_level(smooth, bands, work, out, back, first_row, rows, cols, out_cols, out_rows):
@@ -123,7 +131,7 @@
             work[side, r, pl.ds(0, count, stride=2), :] = even
             work[side, r, pl.ds(1, count, stride=2), :] = odd
 
-    rows_loop(first_row, back + rows, along_y)
+    rows_loop(first_row, back + rows, along_y, UNROLL_B)
     width = 2 * cols + out_cols
 
     def along_x(n):
@@ -135,10 +143,10 @@
             e = LOW_TAPS[2 * t] * s + HIGH_TAPS[2 * t] * d
             o = LOW_TAPS[2 * t + 1] * s + HIGH_TAPS[2 * t + 1] * d
             even, odd = (e, o) if t == 0 else (even + e, odd + o)
-        out[2 * n, 0:width, :] = even
-        out[2 * n + 1, 0:width, :] = odd
-
-    rows_loop(0, rows + out_rows // 2, along_x)
+        out[2 * n, 0:width, :] = even[:, :out.shape[2]]
+        out[2 * n + 1, 0:width, :] = odd[:, :out.shape[2]]
+
+    rows_loop(0, rows + out_rows // 2, along_x, UNROLL_A)
 
 
 def turn(ref, row, steps, planes):
@@ -146,13 +154,38 @@
     return jnp.concatenate([slab, jnp.zeros((LANES - planes, slab.shape[1]), jnp.float32)]).T
 
 
+def lane_of(rows):
+    return lax.broadcasted_iota(jnp.int32, (rows, LANES), 1)
+
+
+def pack(values, heights):
+    flat = values.reshape(-1, LANES)
+    quarter, piece = flat.shape[0] // 4, -(-heights // 3)
+    kept = LANES - piece
+    lane, last = lane_of(quarter), flat[3 * quarter:]
+    return jnp.stack([
+        jnp.where(lane < kept, flat[i * quarter:(i + 1) * quarter], pltpu.roll(last, (kept - piece * i) % LANES, 1))
+        for i in range(3)])
+
+
+def unpack(packed, heights, shape):
+    quarter, piece = packed.shape[1], -(-heights // 3)
+    kept = LANES - piece
+    lane, last = lane_of(quarter), jnp.zeros((quarter, LANES), jnp.float32)
+    for i in range(3):
+        back = pltpu.roll(packed[i], (LANES + piece * i - kept) % LANES, 1)
+        last = jnp.where((lane >= piece * i) & (lane < piece * (i + 1)), back, last)
+    first = [jnp.where(lane < kept, packed[i], 0.0) for i in range(3)]
+    return jnp.concatenate(first + [last]).reshape(shape)
+
+
 def fill(ref):
     ref[...] = jnp.zeros(ref.shape, jnp.float32)
 
 
 def kernel(nx, ny, X, Y, back_x, back_y, inc, cov, out, *scratch):
     (raw, raw_ahead, a0, a1, a2, a3, m1, m2, m3, s4, m4, g4, e4, e5, top, m5, m6, r6, r5, r4, r4l, r3, r2, r1,
-     work, load_sem, a_send, a_recv, m_send, m_recv, s_send, s_recv, g_send, g_recv, pair_send, pair_recv) = scratch
+     work, load_sem, a_send, a_recv, m_send, m_recv, s_send, s_recv, g_send, g_recv, pair_send, pair_recv, *boxes) = scratch
     approx = (a0, a1, a2, a3)
     mixed = {1: m1, 2: m2, 3: m3}
     gx, gy = lax.axis_index("gx"), lax.axis_index("gy")
@@ -224,14 +257,26 @@
 
         return arrive
 
+    def move_packed(box, source, target, send_sem, recv_sem, dx, dy):
+        box[0] = pack(source[...], heights)
+
+        def present():
+            target[...] = unpack(box[1], heights, target.shape)
+
+        return move(box.at[0], box.at[1], send_sem, recv_sem, dx, dy, lambda: fill(target), present)
+
     def send_ahead(level):
         ref, n, w = approx[level], X[level], Y[level]
         own = ((slice(0, AHEAD), slice(0, w)), (slice(0, n), slice(0, COLS)), (slice(0, AHEAD), slice(0, COLS)))
         put = ((slice(n, n + AHEAD), slice(0, w)), (slice(0, n), slice(w, w + COLS)),
                (slice(n, n + AHEAD), slice(w, w + COLS)))
         way = ((-1, 0), (0, -1), (-1, -1))
-        return [move(ref.at[own[i]], ref.at[put[i]], a_send.at[3 * level + i], a_recv.at[3 * level + i], *way[i])
-                for i in range(1 if level == 0 else 0, 3)]
+        steps = [move(ref.at[own[i]], ref.at[put[i]], a_send.at[3 * level + i], a_recv.at[3 * level + i], *way[i])
+                 for i in range(1, 3)]
+        if level:
+            steps.append(move_packed(boxes[level - 1], ref.at[own[0]], ref.at[put[0]],
+                                     a_send.at[3 * level], a_recv.at[3 * level], *way[0]))
+        return steps
 
     def send_back(level):
         ref, n, w, b, s = mixed[level], X[level], Y[level], BACK[level], SENT[level]
@@ -244,8 +289,9 @@
                (every, slice(b - s, b), slice(0, COLS)))
         way = ((1, 0), (0, 1), (1, 1))
         base = 3 * (level - 1)
-        return [move(ref.at[own[i]], ref.at[put[i]], m_send.at[base + i], m_recv.at[base + i], *way[i])
-                for i in range(3)]
+        return [move_packed(boxes[2 + level], ref.at[own[0]], ref.at[put[0]], m_send.at[base], m_recv.at[base], *way[0])
+                ] + [move(ref.at[own[i]], ref.at[put[i]], m_send.at[base + i], m_recv.at[base + i], *way[i])
+                     for i in range(1, 3)]
 
     def turn_ahead():
         for r in range(AHEAD):
@@ -258,7 +304,7 @@
     def turn_own(r):
         a0[r, 0:Y[0], :] = turn(raw, r, X[0], planes)
 
-    rows_loop(0, X[0], turn_own)
+    rows_loop(0, X[0], turn_own, UNROLL_T)
     arrivals = send_ahead(0) + [first]
     late = {}
     for level in range(1, HANDOVER + 1):
@@ -401,9 +447,7 @@
     X += [wide_x // 2, wide_x // 4]
     Y += [wide_y // 2, wide_y // 4]
     back_x, back_y = BACK[4] // X[4], COLS // Y[4]
-    extra = LANES - heights
     planes = -(-heights // 8) * 8
-    turned = jnp.pad(jnp.transpose(covariances, (0, 2, 1)), ((0, 0), (0, extra), (0, extra)))
 
     f32 = functools.partial(pltpu.VMEM, dtype=jnp.float32)
 
@@ -415,6 +459,9 @@
 
     def three(l):
         return f32((3, BACK[l] + X[l], COLS + Y[l], LANES))
+
+    def box(rows, l):
+        return f32((2, 3, rows * Y[l] // 4, LANES))
 
     slots = (back_x + 1) * (back_y + 1)
     work_rows = max(X[1] + BACK[1], X[5] + BACK[5])
@@ -434,17 +481,18 @@
         f32((2, work_rows, work_cols, LANES)),
         dma, dma((12,)), dma((12,)), dma((9,)), dma((9,)), dma((slots,)), dma((slots,)),
         dma((nx * ny // 2,)), dma((nx * ny // 2,)), dma, dma,
+        box(AHEAD, 1), box(AHEAD, 2), box(AHEAD, 3), box(3 * SENT[1], 1), box(3 * SENT[2], 2), box(3 * SENT[3], 3),
     ]
     result = pl.pallas_call(
         functools.partial(kernel, nx, ny, X, Y, back_x, back_y),
-        out_shape=jax.ShapeDtypeStruct((block_x, block_y, LANES), jnp.float32),
+        out_shape=jax.ShapeDtypeStruct((block_x, block_y, heights), jnp.float32),
         in_specs=[pl.BlockSpec(memory_space=pl.ANY), pl.BlockSpec(memory_space=pltpu.VMEM)],
         out_specs=pl.BlockSpec(memory_space=pltpu.VMEM),
         scratch_shapes=scratch,
         compiler_params=pltpu.CompilerParams(
             collective_id=0, has_side_effects=True, vmem_limit_bytes=48 * 1024 * 1024),
-    )(increment[0], turned)
-    return jnp.transpose(result[:, :, :heights], (2, 0, 1))[None]
+    )(increment[0], covariances)
+    return jnp.transpose(result, (2, 0, 1))[None]
 
 
 def solution(mesh):

time: 81.3 us -> 68.8 us (0.85); the launches traced: 81 us -> 67.6 us
  Pallas kernels: 71.7 us -> 61.3 us
  local copies, waits for them, and re-layouts: 9.25 us -> 6.23 us
    pallas_call x1, Pallas kernels: 71.7 us -> 61.3 us  [per_device(): pl.pallas_call(functools.partial(kernel, nx, ny, X, Y, back_x, back_y), o...]
    broadcast_in_dim x2 -> x1, local copies, waits for them, and re-layouts: 7.36 us -> 3.42 us  [per_device(): return jnp.transpose(result, (2, 0, 1))[None]]
    unnamed x3 -> x4, local copies, waits for them, and re-layouts: 1.76 us -> 2.81 us
where the time goes in v2:
time: 68.8 us; the launch traced here: 67.6 us
  Pallas kernels  61.3 us (89%)
  local copies, waits for them, and re-layouts  6.23 us (9%)
    pallas_call x1, Pallas kernels, per_device(): pl.pallas_call(functools.partial(kernel, nx, ny, X, Y, back_x, back_y), o...  61.3 us
    broadcast_in_dim x1, local copies, waits for them, and re-layouts, per_device(): return jnp.transpose(result, (2, 0, 1))[None]  3.42 us
    unnamed x4, local copies, waits for them, and re-layouts  2.81 us

profile of v2, /device:TPU:31, one launch (start us, length us, event | category | flops | bytes accessed | tf_op | source)
XLA Modules:
  0.0 67.6 jit_solution(1974340733966119217)
XLA Ops:
  0.0 0.0 copy-start
  0.0 1.6 %copy-done = f32[1,90,48,128]{3,2,1,0:T(8,128)S(1)} copy-done((f32[1,90,48,128]{3,2,1,0:T(8,128)S(1)}, f32[1,90,48,128]{3,2,1,0:T(8,128)}, u32[]{:S(2)}) %copy-start) | copy-done | bytes 2211864
  1.6 0.0 copy-start.1
  1.6 1.2 %copy-done.1 = f32[19,90,90]{2,1,0:T(8,128)S(1)} copy-done((f32[19,90,90]{2,1,0:T(8,128)S(1)}, f32[19,90,90]{2,1,0:T(8,128)}, u32[]{:S(2)}) %copy-start.1) | copy-done | bytes 615624
  2.8 61.3 %shard_map.28 = f32[48,128,90]{2,1,0:T(8,128)} custom-call(f32[90,48,128]{2,1,0:T(8,128)S(1)} %bitcast.4, f32[19,90,90]{2,1,0:T(8,128)S(1)} %copy-done.1), custom_call_target="tpu_custom_call" | custom-call | tf_op jit(solution)/shard_map/pallas_call | solution.py:486
  64.1 3.4 %copy.3 = f32[1,90,48,128]{3,2,1,0:T(8,128)} copy(f32[1,90,48,128]{1,3,2,0:T(8,128)} %bitcast.5) | data formatting | bytes 4423680 | tf_op jit(solution)/shard_map/broadcast_in_dim | solution.py:495
Async XLA Ops:
  0.0 1.6 %copy-start = (f32[1,90,48,128]{3,2,1,0:T(8,128)S(1)}, f32[1,90,48,128]{3,2,1,0:T(8,128)}, u32[]{:S(2)}) copy-start(f32[1,90,48,128]{3,2,1,0:T(8,128)} %param.2) | copy-start | bytes 6635524
  1.6 1.2 %copy-start.1 = (f32[19,90,90]{2,1,0:T(8,128)S(1)}, f32[19,90,90]{2,1,0:T(8,128)}, u32[]{:S(2)}) copy-start(f32[19,90,90]{2,1,0:T(8,128)} %cov.1) | copy-start | bytes 1846804

commit v3 on v2

--- a/solution.py
+++ b/solution.py
@@ -52,17 +52,17 @@
         body(r)
 
 
-def split_rows(source, work, rows, cols):
+def split_rows(source, work, rows, first, cols):
     def body(k):
         smooth = detail = None
         for j in range(8):
-            row = source[2 * k + j, 0:cols, :]
+            row = source[2 * k + j, first:cols, :]
             if j == 0:
                 smooth, detail = LOW_TAPS[j] * row, HIGH_TAPS[j] * row
             else:
                 smooth, detail = smooth + LOW_TAPS[j] * row, detail + HIGH_TAPS[j] * row
-        work[0, k, 0:cols, :] = smooth
-        work[1, k, 0:cols, :] = detail
+        work[0, k, first:cols, :] = smooth
+        work[1, k, first:cols, :] = detail
 
     rows_loop(0, rows, body, UNROLL_A)
 
@@ -267,31 +267,31 @@
 
     def send_ahead(level):
         ref, n, w = approx[level], X[level], Y[level]
-        own = ((slice(0, AHEAD), slice(0, w)), (slice(0, n), slice(0, COLS)), (slice(0, AHEAD), slice(0, COLS)))
-        put = ((slice(n, n + AHEAD), slice(0, w)), (slice(0, n), slice(w, w + COLS)),
-               (slice(n, n + AHEAD), slice(w, w + COLS)))
-        way = ((-1, 0), (0, -1), (-1, -1))
-        steps = [move(ref.at[own[i]], ref.at[put[i]], a_send.at[3 * level + i], a_recv.at[3 * level + i], *way[i])
-                 for i in range(1, 3)]
+        s = 3 * level
+        cols = move(ref.at[0:n, 0:COLS], ref.at[0:n, w:w + COLS], a_send.at[s + 1], a_recv.at[s + 1], 0, -1)
+        rows = None
         if level:
-            steps.append(move_packed(boxes[level - 1], ref.at[own[0]], ref.at[put[0]],
-                                     a_send.at[3 * level], a_recv.at[3 * level], *way[0]))
-        return steps
+            rows = move_packed(boxes[level - 1], ref.at[0:AHEAD, 0:w], ref.at[n:n + AHEAD, 0:w],
+                               a_send.at[s], a_recv.at[s], -1, 0)
+        return rows, cols
+
+    def corner_ahead(level):
+        ref, n, w = approx[level], X[level], Y[level]
+        s = 3 * level + 2
+        return move(ref.at[n:n + AHEAD, 0:COLS], ref.at[n:n + AHEAD, w:w + COLS], a_send.at[s], a_recv.at[s], 0, -1)
 
     def send_back(level):
         ref, n, w, b, s = mixed[level], X[level], Y[level], BACK[level], SENT[level]
-        every = slice(0, 3)
-        own = ((every, slice(b + n - s, b + n), slice(COLS, COLS + w)),
-               (every, slice(b, b + n), slice(w, w + COLS)),
-               (every, slice(b + n - s, b + n), slice(w, w + COLS)))
-        put = ((every, slice(b - s, b), slice(COLS, COLS + w)),
-               (every, slice(b, b + n), slice(0, COLS)),
-               (every, slice(b - s, b), slice(0, COLS)))
-        way = ((1, 0), (0, 1), (1, 1))
-        base = 3 * (level - 1)
-        return [move_packed(boxes[2 + level], ref.at[own[0]], ref.at[put[0]], m_send.at[base], m_recv.at[base], *way[0])
-                ] + [move(ref.at[own[i]], ref.at[put[i]], m_send.at[base + i], m_recv.at[base + i], *way[i])
-                     for i in range(1, 3)]
+        k = 3 * (level - 1)
+        rows = move_packed(boxes[2 + level], ref.at[:, b + n - s:b + n, COLS:COLS + w],
+                           ref.at[:, b - s:b, COLS:COLS + w], m_send.at[k], m_recv.at[k], 1, 0)
+        cols = move(ref.at[:, b:b + n, w:w + COLS], ref.at[:, b:b + n, 0:COLS], m_send.at[k + 1], m_recv.at[k + 1], 0, 1)
+        return rows, cols
+
+    def corner_back(level):
+        ref, w, b, s = mixed[level], Y[level], BACK[level], SENT[level]
+        k = 3 * (level - 1) + 2
+        return move(ref.at[:, b - s:b, w:w + COLS], ref.at[:, b - s:b, 0:COLS], m_send.at[k], m_recv.at[k], 0, 1)
 
     def turn_ahead():
         for r in range(AHEAD):
@@ -305,13 +305,17 @@
         a0[r, 0:Y[0], :] = turn(raw, r, X[0], planes)
 
     rows_loop(0, X[0], turn_own, UNROLL_T)
-    arrivals = send_ahead(0) + [first]
+    arrivals = (first, send_ahead(0)[1])
     late = {}
     for level in range(1, HANDOVER + 1):
-        for arrive in arrivals:
-            arrive()
         rows, cols = X[level], Y[level]
-        split_rows(approx[level - 1], work, rows, Y[level - 1] + COLS)
+        own = Y[level - 1]
+        arrivals[0]()
+        corner = corner_ahead(level - 1)
+        split_rows(approx[level - 1], work, rows, 0, own)
+        arrivals[1]()
+        corner()
+        split_rows(approx[level - 1], work, rows, own, own + COLS)
         if level < HANDOVER:
             target, bands, b = approx[level], mixed[level], BACK[level]
 
@@ -327,7 +331,7 @@
             arrivals = send_ahead(level)
             for band in range(3):
                 mix(bands, band, cov, 3 * (level - 1) + band, b, rows, COLS, cols)
-            late[level] = send_back(level)
+            pass
         else:
             own4 = s4.at[0]
             if Y4 != COLS:
@@ -364,18 +368,24 @@
 
     for band in range(3):
         mix(s4.at[0], band, cov, 3 * (HANDOVER - 1) + band, 0, X4, 0, COLS)
-    late4 = []
-    for dx in range(back_x + 1):
-        for dy in range(back_y + 1):
-            if dx or dy:
-                slot = dx * (back_y + 1) + dy
-                late4.append(move(s4.at[0], s4.at[slot], s_send.at[slot], s_recv.at[slot], dx, dy))
+    def block(dx, dy):
+        slot, source = dx * (back_y + 1) + dy, dx * (back_y + 1) if dy else 0
+        return move(s4.at[source], s4.at[slot], s_send.at[slot], s_recv.at[slot], 0 if dy else dx, dy)
+
+    behind_x = [block(dx, 0) for dx in range(1, back_x + 1)]
+    late4 = [block(0, dy) for dy in range(1, back_y + 1)]
 
     for ref in (e4, e5, m5, m6, r6):
         fill(ref)
+    for level in (3, 2, 1):
+        late[level] = send_back(level)
     rows_loop(1, chips, lambda o: landed(o).wait_recv())
     pair(core).start()
     pair(1 - core).wait_recv()
+
+    for dx in range(1, back_x + 1):
+        behind_x[dx - 1]()
+        late4 += [block(dx, dy) for dy in range(1, back_y + 1)]
 
     def assemble(px):
         for py in range(ny):
@@ -387,7 +397,7 @@
     for level, source, target, bands in ((5, e4, e5, m5), (6, e5, top, m6)):
         rows, cols = X[level], Y[level]
         b = BACK[level]
-        split_rows(source, work, rows, 2 * cols + COLS)
+        split_rows(source, work, rows, 0, 2 * cols + COLS)
 
         def put(side, k, smooth, detail, target=target, bands=bands, b=b, cols=cols):
             if side == 0:
@@ -408,6 +418,11 @@
     merge_level(top.at[0], m6, work, r5, BACK[6], 0, X[6], Y[6], COLS, BACK[5])
     merge_level(r5, m5, work, r4, BACK[5], 0, X[5], Y[5], COLS, BACK[4])
 
+    def forward(level):
+        late[level][0]()
+        late[level] = (late[level][1], corner_back(level))
+
+    forward(3)
     for py in range(ny):
         @pl.when(gy == py)
         def _():
@@ -426,6 +441,8 @@
 
     merge_level(r4l, m4, work, r3, BACK[4], 0, X4, Y4, COLS, BACK[3])
     for level, source, target in ((3, r3, r2), (2, r2, r1), (1, r1, out)):
+        if level > 1:
+            forward(level - 1)
         for arrive in late[level]:
             arrive()
         final = level == 1

time: 68.8 us -> 65 us (0.945)
  the two profiles are of different devices: /device:TPU:31 before, /device:TPU:16 now
where the time goes in v3:
time: 65 us; the launch traced here: 64.9 us
  Pallas kernels  58.6 us (90%)
  local copies, waits for them, and re-layouts  6.23 us (10%)
    pallas_call x1, Pallas kernels, per_device(): pl.pallas_call(functools.partial(kernel, nx, ny, X, Y, back_x, back_y), o...  58.6 us
    broadcast_in_dim x1, local copies, waits for them, and re-layouts, per_device(): return jnp.transpose(result, (2, 0, 1))[None]  3.42 us
    unnamed x4, local copies, waits for them, and re-layouts  2.81 us

profile of v3, /device:TPU:16, one launch (start us, length us, event | category | flops | bytes accessed | tf_op | source)
XLA Modules:
  0.0 64.9 jit_solution(11225361955434115871)
XLA Ops:
  0.0 0.0 copy-start
  0.0 1.6 %copy-done = f32[1,90,48,128]{3,2,1,0:T(8,128)S(1)} copy-done((f32[1,90,48,128]{3,2,1,0:T(8,128)S(1)}, f32[1,90,48,128]{3,2,1,0:T(8,128)}, u32[]{:S(2)}) %copy-start) | copy-done | bytes 2211864
  1.6 0.0 copy-start.1
  1.6 1.2 %copy-done.1 = f32[19,90,90]{2,1,0:T(8,128)S(1)} copy-done((f32[19,90,90]{2,1,0:T(8,128)S(1)}, f32[19,90,90]{2,1,0:T(8,128)}, u32[]{:S(2)}) %copy-start.1) | copy-done | bytes 615624
  2.8 58.6 %shard_map.28 = f32[48,128,90]{2,1,0:T(8,128)} custom-call(f32[90,48,128]{2,1,0:T(8,128)S(1)} %bitcast.4, f32[19,90,90]{2,1,0:T(8,128)S(1)} %copy-done.1), custom_call_target="tpu_custom_call" | custom-call | tf_op jit(solution)/shard_map/pallas_call | solution.py:503
  61.4 3.4 %copy.3 = f32[1,90,48,128]{3,2,1,0:T(8,128)} copy(f32[1,90,48,128]{1,3,2,0:T(8,128)} %bitcast.5) | data formatting | bytes 4423680 | tf_op jit(solution)/shard_map/broadcast_in_dim | solution.py:512
Async XLA Ops:
  0.0 1.6 %copy-start = (f32[1,90,48,128]{3,2,1,0:T(8,128)S(1)}, f32[1,90,48,128]{3,2,1,0:T(8,128)}, u32[]{:S(2)}) copy-start(f32[1,90,48,128]{3,2,1,0:T(8,128)} %param.2) | copy-start | bytes 6635524
  1.6 1.2 %copy-start.1 = (f32[19,90,90]{2,1,0:T(8,128)S(1)}, f32[19,90,90]{2,1,0:T(8,128)}, u32[]{:S(2)}) copy-start(f32[19,90,90]{2,1,0:T(8,128)} %cov.1) | copy-start | bytes 1846804
